TPU v7x, 32 devices: a whole 2x2x4 slice. The times are simulated.
32 devices in a mesh: gx: 8 (over y, x, core), node: 4 (over z).
Axes of the slice: x: 2, y: 2, z: 4, core: 2. Of those that a mesh axis runs over, the one named last changes fastest.
Arguments:
- logfield: bfloat16 [4, 64, 1024, 256], P('node', 'gx'), may hold values from -4 to 4
- state: float32 [4, 64, 1024, 256], P('node', 'gx'), may hold values from -48 to 48
- target: float32 [64, 1024, 256], P('gx'), may hold values from -48 to 48
- node_index: int32 [4], P('node'), may hold values from 0 to 8
- weight_numer: int32 [4], P('node'), may hold values from 1 to 16
Outputs:
- riesz_gradient: float32 [64, 1024, 256], P('gx', 'node')
Inputs may be any that keep to these rules, and one draw needn't show every extreme that they name: `node_index`: index i stands for the abscissa cos(pi i / 8). `weight_numer`: the node's weight is the numerator over 8.
All inputs are finite; a program needn't handle non-finite values.
Results may differ from a plain program's by a relative error of at most 0.0003.
Values may be sent and summed in bfloat16 or wider, within the bound.
A program may use at most 320 MiB of HBM per device.

v0:
```python
import math

import jax
import jax.numpy as jnp
from jax import lax
from jax.sharding import PartitionSpec as P

SMOOTH_SWEEPS = 2


relax = 2.0 / 3.0
riesz_beta = 1.0


def extended(cells, sides, width):
    for axis, dim in sides:
        count = lax.axis_size(axis)
        head = lax.slice_in_dim(cells, 0, width, axis=dim)
        tail = lax.slice_in_dim(cells, cells.shape[dim] - width, cells.shape[dim], axis=dim)
        cells = jnp.concatenate(
            [
                lax.ppermute(tail, axis, [(i, (i + 1) % count) for i in range(count)]),
                cells,
                lax.ppermute(head, axis, [((i + 1) % count, i) for i in range(count)]),
            ],
            axis=dim,
        )
    return cells


def face_terms(kappa_ext):
    center = kappa_ext[1:-1]
    padded_y = jnp.pad(center, ((0, 0), (1, 1), (0, 0)), mode="edge")
    padded_z = jnp.pad(center, ((0, 0), (0, 0), (1, 1)), mode="edge")
    coefs = (
        0.5 * (center + kappa_ext[:-2]),
        0.5 * (center + kappa_ext[2:]),
        0.5 * (center + padded_y[:, :-2]),
        0.5 * (center + padded_y[:, 2:]),
        0.5 * (center + padded_z[:, :, :-2]),
        0.5 * (center + padded_z[:, :, 2:]),
    )
    diagonal = coefs[0] + coefs[1] + coefs[2] + coefs[3] + coefs[4] + coefs[5]
    return (coefs, diagonal)


def neighbour_sum(coefs, value_ext):
    center = value_ext[1:-1]
    padded_y = jnp.pad(center, ((0, 0), (1, 1), (0, 0)))
    padded_z = jnp.pad(center, ((0, 0), (0, 0), (1, 1)))
    return (
        coefs[0] * value_ext[:-2]
        + coefs[1] * value_ext[2:]
        + coefs[2] * padded_y[:, :-2]
        + coefs[3] * padded_y[:, 2:]
        + coefs[4] * padded_z[:, :, :-2]
        + coefs[5] * padded_z[:, :, 2:]
    )


def jacobi_step(previous_ext, misfit, coefs, diagonal):
    center = previous_ext[1:-1]
    image = diagonal * center - neighbour_sum(coefs, previous_ext)
    return center + relax * (misfit - image) / diagonal


def riesz_step(smooth_ext, source):
    center = smooth_ext[1:-1, 1:-1]
    padded_z = jnp.pad(center, ((0, 0), (0, 0), (1, 1)))
    beside_all = (
        smooth_ext[:-2, 1:-1]
        + smooth_ext[2:, 1:-1]
        + smooth_ext[1:-1, :-2]
        + smooth_ext[1:-1, 2:]
        + padded_z[:, :, :-2]
        + padded_z[:, :, 2:]
    )
    return (source + riesz_beta * beside_all) / (1.0 + 6.0 * riesz_beta)


def per_device(logfield, state, target, node_index, weight_numer):
    field = logfield[0]
    misfit = state[0] - target
    abscissa = jnp.cos(math.pi * node_index[0].astype(jnp.float32) / 8.0)
    field_ext = extended(field, (("gx", 0),), 1)
    kappa_ext = jnp.exp(0.5 * abscissa * field_ext.astype(jnp.float32))
    coefs, diagonal = face_terms(kappa_ext)
    adjoint = relax * misfit / diagonal
    adjoint_ext = extended(adjoint, (("gx", 0),), 1)
    adjoint = jacobi_step(adjoint_ext, misfit, coefs, diagonal)
    weight = weight_numer[0].astype(jnp.float32) / 8.0
    term = weight * adjoint
    total = lax.psum(term, "node")
    piece_rows = total.shape[1] // lax.axis_size("node")
    gradient = lax.dynamic_slice_in_dim(total, lax.axis_index("node") * piece_rows, piece_rows, 1)
    position = lax.axis_index("node")
    first_piece = position == 0
    last_piece = position == lax.axis_size("node") - 1
    row_ids = jnp.arange(gradient.shape[1] + 2)
    outside = (row_ids == 0) & first_piece | (row_ids == gradient.shape[1] + 1) & last_piece
    smooth = gradient
    for sweep in range(SMOOTH_SWEEPS):
        smooth_ext = extended(smooth, (("gx", 0), ("node", 1)), 1)
        smooth_ext = jnp.where(outside[None, :, None], jnp.float32(0.0), smooth_ext)
        smooth = riesz_step(smooth_ext, gradient)
    return smooth


def solution(mesh):
    in_specs = (
        P("node", "gx", None, None),
        P("node", "gx", None, None),
        P("gx", None, None),
        P("node"),
        P("node"),
    )
    out_specs = P("gx", "node", None)
    return jax.shard_map(
        per_device, mesh=mesh, in_specs=in_specs, out_specs=out_specs, check_vma=False
    )
```

profile of v0, /device:TPU:0, one launch (start us, length us, event | category | flops | bytes accessed | tf_op | source)
XLA Modules:
  0.0 483.3 jit_solution(8810282573691941032)
XLA Ops:
  6.5 1.3 slice_bitcast_fusion.1
  7.8 0.5 collective-permute-start
  8.3 2.9 collective-permute-start.1
  12.0 9.0 %collective-permute-done = bf16[1,1024,256]{2,1,0:T(8,128)(2,1)S(1)} collective-permute-done((bf16[1,1024,256]{2,1,0:T(8,128)(2,1)S(1)}, bf16[1,1024,256]{2,1,0:T(8,128)(2,1)S(1)}, u32[]{:S(2)}, u32[]{:S(2)}) %collective-permute-start) | collective-permute-done | bytes 524320 | tf_op jit(solution)/shard_map/ppermute | solution.py:22
  21.0 1.5 collective-permute-done.1
  22.5 3.7 multiply_exponential_fusion
  26.2 4.0 fusion.37
  30.2 1.3 copy-done
  31.5 4.0 slice.194
  35.5 33.2 %fusion.24 = f32[8,1024,256]{2,1,0:T(8,128)} fusion(f32[8,1024,256]{2,1,0:T(8,128)} %slice.194, f32[8,1,256]{2,1,0:T(1,128)S(1)} %get-tuple-element.8, f32[8,1,256]{2,1,0:T(1,128)S(1)} %get-tuple-element.7, f32[8,1024,1]{2,1,0:T(8,128)} %get-tuple-element.6, f32[8,1024,1]{2,1,0:T(8,128)S(1)} %get-tuple-element.5, f32[10,1024,256]{2,1,0:T(8,128)} %copy-done, ...), kind=kLoop, calls=%fused_computation.37 | loop fusion | flops 50331648 | bytes 50413568 | tf_op jit(solution)/shard_map/div | solution.py:88
  68.7 1.7 fusion.39
  70.4 1.8 collective-permute-start.2
  72.2 1.1 collective-permute-start.3
  74.0 22.1 %collective-permute-done.2 = f32[1,1024,256]{2,1,0:T(8,128)S(1)} collective-permute-done((f32[1,1024,256]{2,1,0:T(8,128)S(1)}, f32[1,1024,256]{2,1,0:T(8,128)S(1)}, u32[]{:S(2)}, u32[]{:S(2)}) %collective-permute-start.2) | collective-permute-done | bytes 1048608 | tf_op jit(solution)/shard_map/ppermute | solution.py:22
  96.1 50.8 %fusion.25 = f32[8,1024,256]{2,1,0:T(8,128)} fusion(f32[8,1024,256]{2,1,0:T(8,128)} %fusion.24, f32[1,1024,256]{2,1,0:T(8,128)S(1)} %collective-permute-done.3, f32[1,1024,256]{2,1,0:T(8,128)S(1)} %collective-permute-done.2, f32[8,1024,256]{2,1,0:T(8,128)} %slice.194, f32[8,1,256]{2,1,0:T(1,128)S(1)} %get-tuple-element.8, ...), kind=kLoop, calls=%fused_computation.38 | loop fusion | flops 88080384 | bytes 60899332 | tf_op jit(solution)/shard_map/mul | solution.py:92
  147.0 293.1 %all-reduce.6.cloned.1.call-done = f32[8,1024,256]{2,1,0:T(8,128)} async-done(((f32[8,1024,256]{2,1,0:T(8,128)}), f32[8,1024,256]{2,1,0:T(8,128)}) %all-reduce.6.cloned.1.call-update) | async-done | bytes 8388624 | tf_op jit(solution)/shard_map/psum | solution.py:93
  440.0 1.1 constant_dynamic-slice_fusion.1
  441.1 2.6 collective-permute-start.5
  443.8 1.8 constant_dynamic-slice_fusion.2
  445.6 3.2 collective-permute-done.4
  448.9 3.8 collective-permute-start.7
  452.7 1.6 collective-permute-done.6
  454.3 0.3 maximum_select_fusion
  454.9 2.8 fusion.29
  457.7 0.6 collective-permute-start.8
  458.3 2.0 collective-permute-start.9
  460.4 5.8 %collective-permute-done.8 = f32[1,256,256]{2,1,0:T(8,128)S(1)} collective-permute-done((f32[1,256,256]{2,1,0:T(8,128)S(1)}, f32[1,256,256]{2,1,0:T(8,128)S(1)}, u32[]{:S(2)}, u32[]{:S(2)}) %collective-permute-start.8) | collective-permute-done | bytes 262176 | tf_op jit(solution)/shard_map/ppermute | solution.py:22
  466.2 0.5 collective-permute-start.10
  466.7 3.6 collective-permute-start.11
  470.2 1.6 collective-permute-done.10
  471.8 0.4 maximum_select_fusion.1
  472.4 4.1 fusion.33
  (19 shorter events, 0.7 us)
Async XLA Ops:
  6.5 433.5 %all-reduce.6.cloned.1.call-start = ((), (), s32[]{:S(2)}) async-start(), calls=%async_computation | async-start | bytes 16777216 | tf_op jit(solution)/shard_map/psum | solution.py:93
  7.8 13.2 %collective-permute-start = (bf16[1,1024,256]{2,1,0:T(8,128)(2,1)S(1)}, bf16[1,1024,256]{2,1,0:T(8,128)(2,1)S(1)}, u32[]{:S(2)}, u32[]{:S(2)}) collective-permute-start(bf16[1,1024,256]{2,1,0:T(8,128)(2,1)S(1)} %get-tuple-element.13), channel_id=1, source_target_pairs={{0,4},{4,8},{8,12},{12,16},{16,20},{20,24},{24,28},{28,0},{1,5},{5... | collective-permute-start | bytes 1572872 | tf_op jit(solution)/shard_map/ppermute | solution.py:22
  8.3 14.2 %collective-permute-start.1 = (bf16[1,1024,256]{2,1,0:T(8,128)(2,1)S(1)}, bf16[1,1024,256]{2,1,0:T(8,128)(2,1)S(1)}, u32[]{:S(2)}, u32[]{:S(2)}) collective-permute-start(bf16[1,1024,256]{2,1,0:T(8,128)(2,1)S(1)} %get-tuple-element.14), channel_id=1, source_target_pairs={{4,0},{8,4},{12,8},{16,12},{20,16},{24,20},{28,24},{0,28},{5,1},{9... | collective-permute-start | bytes 1572872 | tf_op jit(solution)/shard_map/ppermute | solution.py:24
  26.2 5.3 %copy-start = (f32[10,1024,256]{2,1,0:T(8,128)}, f32[10,1024,256]{2,1,0:T(8,128)S(1)}, u32[]{:S(2)}) copy-start(f32[10,1024,256]{2,1,0:T(8,128)S(1)} %multiply_exponential_fusion) | copy-start | bytes 31457284
  30.2 5.3 %copy-start.1 = (f32[8,1024,1]{2,1,0:T(8,128)}, f32[8,1024,1]{2,1,0:T(8,128)S(1)}, u32[]{:S(2)}) copy-start(f32[8,1024,1]{2,1,0:T(8,128)S(1)} %get-tuple-element.5) | copy-start | bytes 98308
  70.4 25.7 %collective-permute-start.2 = (f32[1,1024,256]{2,1,0:T(8,128)S(1)}, f32[1,1024,256]{2,1,0:T(8,128)S(1)}, u32[]{:S(2)}, u32[]{:S(2)}) collective-permute-start(f32[1,1024,256]{2,1,0:T(8,128)S(1)} %get-tuple-element.11), channel_id=1, source_target_pairs={{0,4},{4,8},{8,12},{12,16},{16,20},{20,24},{24,28},{28,0},{1,5},{5... | collective-permute-start | bytes 3145736 | tf_op jit(solution)/shard_map/ppermute | solution.py:22
  72.2 23.9 %collective-permute-start.3 = (f32[1,1024,256]{2,1,0:T(8,128)S(1)}, f32[1,1024,256]{2,1,0:T(8,128)S(1)}, u32[]{:S(2)}, u32[]{:S(2)}) collective-permute-start(f32[1,1024,256]{2,1,0:T(8,128)S(1)} %get-tuple-element.12), channel_id=1, source_target_pairs={{4,0},{8,4},{12,8},{16,12},{20,16},{24,20},{28,24},{0,28},{5,1},{9... | collective-permute-start | bytes 3145736 | tf_op jit(solution)/shard_map/ppermute | solution.py:24
  441.1 7.7 %collective-permute-start.4 = (f32[1,256,256]{2,1,0:T(8,128)S(1)}, f32[1,256,256]{2,1,0:T(8,128)S(1)}, u32[]{:S(2)}, u32[]{:S(2)}) collective-permute-start(f32[1,256,256]{2,1,0:T(8,128)S(1)} %get-tuple-element.9), channel_id=1, source_target_pairs={{0,4},{4,8},{8,12},{12,16},{16,20},{20,24},{24,28},{28,0},{1,5},{5... | collective-permute-start | bytes 786440 | tf_op jit(solution)/shard_map/ppermute | solution.py:22
  441.1 7.6 %collective-permute-start.5 = (f32[1,256,256]{2,1,0:T(8,128)S(1)}, f32[1,256,256]{2,1,0:T(8,128)S(1)}, u32[]{:S(2)}, u32[]{:S(2)}) collective-permute-start(f32[1,256,256]{2,1,0:T(8,128)S(1)} %get-tuple-element.10), channel_id=1, source_target_pairs={{4,0},{8,4},{12,8},{16,12},{20,16},{24,20},{28,24},{0,28},{5,1},{9... | collective-permute-start | bytes 786440 | tf_op jit(solution)/shard_map/ppermute | solution.py:24
  448.8 5.5 %collective-permute-start.6 = (f32[10,1,256]{2,1,0:T(1,128)S(1)}, f32[10,1,256]{2,1,0:T(1,128)S(1)}, u32[]{:S(2)}, u32[]{:S(2)}) collective-permute-start(f32[10,1,256]{2,1,0:T(1,128)S(1)} %get-tuple-element.17), channel_id=1, source_target_pairs={{0,1},{1,2},{2,3},{3,0},{4,5},{5,6},{6,7},{7,4},{8,9},{9,10},{10,1... | collective-permute-start | bytes 30728 | tf_op jit(solution)/shard_map/ppermute | solution.py:22
  448.9 5.5 %collective-permute-start.7 = (f32[10,1,256]{2,1,0:T(1,128)S(1)}, f32[10,1,256]{2,1,0:T(1,128)S(1)}, u32[]{:S(2)}, u32[]{:S(2)}) collective-permute-start(f32[10,1,256]{2,1,0:T(1,128)S(1)} %get-tuple-element.18), channel_id=1, source_target_pairs={{1,0},{2,1},{3,2},{0,3},{5,4},{6,5},{7,6},{4,7},{9,8},{10,9},{11,1... | collective-permute-start | bytes 30728 | tf_op jit(solution)/shard_map/ppermute | solution.py:24
  457.7 8.5 %collective-permute-start.8 = (f32[1,256,256]{2,1,0:T(8,128)S(1)}, f32[1,256,256]{2,1,0:T(8,128)S(1)}, u32[]{:S(2)}, u32[]{:S(2)}) collective-permute-start(f32[1,256,256]{2,1,0:T(8,128)S(1)} %get-tuple-element.19), channel_id=1, source_target_pairs={{0,4},{4,8},{8,12},{12,16},{16,20},{20,24},{24,28},{28,0},{1,5},{5... | collective-permute-start | bytes 786440 | tf_op jit(solution)/shard_map/ppermute | solution.py:22
  458.3 7.9 %collective-permute-start.9 = (f32[1,256,256]{2,1,0:T(8,128)S(1)}, f32[1,256,256]{2,1,0:T(8,128)S(1)}, u32[]{:S(2)}, u32[]{:S(2)}) collective-permute-start(f32[1,256,256]{2,1,0:T(8,128)S(1)} %get-tuple-element.20), channel_id=1, source_target_pairs={{4,0},{8,4},{12,8},{16,12},{20,16},{24,20},{28,24},{0,28},{5,1},{9... | collective-permute-start | bytes 786440 | tf_op jit(solution)/shard_map/ppermute | solution.py:24
  466.2 5.6 %collective-permute-start.10 = (f32[10,1,256]{2,1,0:T(1,128)S(1)}, f32[10,1,256]{2,1,0:T(1,128)S(1)}, u32[]{:S(2)}, u32[]{:S(2)}) collective-permute-start(f32[10,1,256]{2,1,0:T(1,128)S(1)} %get-tuple-element.15), channel_id=1, source_target_pairs={{0,1},{1,2},{2,3},{3,0},{4,5},{5,6},{6,7},{7,4},{8,9},{9,10},{10,1... | collective-permute-start | bytes 30728 | tf_op jit(solution)/shard_map/ppermute | solution.py:22
  466.7 5.1 %collective-permute-start.11 = (f32[10,1,256]{2,1,0:T(1,128)S(1)}, f32[10,1,256]{2,1,0:T(1,128)S(1)}, u32[]{:S(2)}, u32[]{:S(2)}) collective-permute-start(f32[10,1,256]{2,1,0:T(1,128)S(1)} %get-tuple-element.16), channel_id=1, source_target_pairs={{1,0},{2,1},{3,2},{0,3},{5,4},{6,5},{7,6},{4,7},{9,8},{10,9},{11,1... | collective-permute-start | bytes 30728 | tf_op jit(solution)/shard_map/ppermute | solution.py:24
Sparse Core Ops, SparseCore 0:
  147.1 292.8 all-reduce.5
where the time goes:
time: 484 us; the launch traced here: 483 us
  waiting for transfers between devices  338 us (70%)
  other arithmetic  95.2 us (20%)
  starting transfers between devices  19.7 us (4%)
  local copies, waits for them, and re-layouts  15.6 us (3%)
  between operations  14.9 us (3%)
    psum x1, waiting for transfers between devices, per_device(): total = lax.psum(term, 'node')  293 us
    mul x1, other arithmetic, per_device(): term = weight * adjoint  50.8 us
    ppermute x6, waiting for transfers between devices, extended(): lax.ppermute(tail, axis, [(i, (i + 1) % count) for i in range(count)])  43.4 us
    div x1, other arithmetic, per_device(): adjoint = relax * misfit / diagonal  33.2 us
    ppermute x6, starting transfers between devices, extended(): lax.ppermute(head, axis, [((i + 1) % count, i) for i in range(count)])  16.1 us
  transfers between devices with their start and end apart: 13, of which 8 were waited for; matrix products, arithmetic and copies ran while one was open for 0% of the time, Pallas kernels for 0%

commit v1 on v0

v1 whole, which is shorter than its diff:
```python
import functools
import math

import jax
import jax.numpy as jnp
from jax import lax
from jax.experimental import pallas as pl
from jax.experimental.pallas import tpu as pltpu
from jax.sharding import PartitionSpec as P

RELAX = 2.0 / 3.0
BETA = 1.0
TOP = 32767.0
MESH = pl.DeviceIdType.MESH


def rolled(v, by):
    return pltpu.roll(v, by, 1)


def kernel(G, K, X, Y, Z, CH, lf, st, tg, ni, wn, out,
           lfw, stw, tgw, kap, adj, inv, asend, ahalo, term, qs, sc, qr, sr, grad, sm1,
           lf_loc, lf_send, lf_recv, st_sem, tg_sem, a_send, a_recv,
           q_send, q_recv, s_send, s_recv, g_send, g_recv, r_send, r_recv):
    R = Y // K
    C = R // CH
    NC = K * C
    gx = lax.axis_index("gx")
    node = lax.axis_index("node")
    left = lax.rem(gx + G - 1, G)
    right = lax.rem(gx + 1, G)

    barrier = pltpu.get_barrier_semaphore()
    for k in range(K):
        for g in (left, right):
            pl.semaphore_signal(barrier, inc=1, device_id=(g, jnp.int32(k)), device_id_type=MESH)
    for k in range(1, K):
        pl.semaphore_signal(barrier, inc=1, device_id=(gx, lax.rem(node + k, K)), device_id_type=MESH)

    def piece_of(s):
        return lax.rem(node + K - 1 - s // C + K, K)

    def chunk_of(s):
        return piece_of(s) * C + lax.rem(s, C)

    def lf_start(s):
        first = chunk_of(s) * CH
        start = pl.multiple_of(jnp.clip(first - 16, 0, Y - CH - 32), 16)
        dst = pl.multiple_of(32 + start - first, 16)
        return start, dst

    def lf_local(s):
        start, dst = lf_start(s)
        return pltpu.make_async_copy(
            lf.at[0, :, pl.ds(start, CH + 32), :],
            lfw.at[s, pl.ds(1, X), pl.ds(dst, CH + 32), :], lf_loc.at[s])

    def lf_remote(s, side):
        start, dst = lf_start(s)
        src = 0 if side == 1 else X - 1
        to = X + 1 if side == 1 else 0
        return pltpu.make_async_remote_copy(
            src_ref=lf.at[0, src, pl.ds(start, CH + 32), :],
            dst_ref=lfw.at[s, to, pl.ds(dst, CH + 32), :],
            send_sem=lf_send.at[side, s], recv_sem=lf_recv.at[side, s],
            device_id=(left if side == 1 else right, node), device_id_type=MESH)

    def st_copies(s):
        first = chunk_of(s) * CH
        start = pl.multiple_of(jnp.clip(first - 8, 0, Y - CH - 16), 8)
        dst = pl.multiple_of(16 + start - first, 8)
        slot = lax.rem(s, 2)
        return (
            pltpu.make_async_copy(st.at[0, :, pl.ds(start, CH + 16), :],
                                  stw.at[slot, :, pl.ds(dst, CH + 16), :], st_sem.at[slot]),
            pltpu.make_async_copy(tg.at[:, pl.ds(start, CH + 16), :],
                                  tgw.at[slot, :, pl.ds(dst, CH + 16), :], tg_sem.at[slot]))

    def a_remote(s, side):
        return pltpu.make_async_remote_copy(
            src_ref=asend.at[s, 0 if side == 1 else 1],
            dst_ref=ahalo.at[s, side],
            send_sem=a_send.at[side, s], recv_sem=a_recv.at[side, s],
            device_id=(left if side == 1 else right, node), device_id_type=MESH)

    def q_copies(s):
        dest = piece_of(s)
        ci = lax.rem(s, C)
        slot = jnp.where(node < dest, node, node - 1)
        slot = jnp.clip(slot, 0, K - 2)
        return (
            pltpu.make_async_remote_copy(
                src_ref=qs.at[s], dst_ref=qr.at[slot, ci], send_sem=q_send.at[s],
                recv_sem=q_recv.at[slot, ci], device_id=(gx, dest), device_id_type=MESH),
            pltpu.make_async_remote_copy(
                src_ref=sc.at[s], dst_ref=sr.at[slot, ci], send_sem=s_send.at[s],
                recv_sem=s_recv.at[slot, ci], device_id=(gx, dest), device_id_type=MESH))

    index = ni[0]
    half = jnp.float32(0.5 * math.cos(0.0))
    for i in range(1, 9):
        half = jnp.where(index == i, jnp.float32(0.5 * math.cos(math.pi * i / 8)), half)
    weight = wn[0].astype(jnp.float32) / 8.0
    lane = lax.broadcasted_iota(jnp.int32, (16, Z), 1)
    is_first = lane == 0
    is_last = lane == Z - 1

    for s in range(2):
        lf_local(s).start()
    for cp in st_copies(0):
        cp.start()
    pl.semaphore_wait(barrier, 3 * K - 1)
    for s in range(2):
        for side in range(2):
            lf_remote(s, side).start()

    def phase1(s):
        slot = lax.rem(s, 2)
        c = chunk_of(s)

        @pl.when(s + 2 < NC)
        def _():
            lf_local(s + 2).start()
            for side in range(2):
                lf_remote(s + 2, side).start()

        @pl.when(s + 1 < NC)
        def _():
            for cp in st_copies(s + 1):
                cp.start()

        lf_local(s).wait()
        for side in range(2):
            lf_remote(s, side).wait_recv()

        def kappa(p, _):
            for r in range(16, CH + 48, 16):
                kap[slot, p, r:r + 16, :] = jnp.exp(half * lfw[s, p, r:r + 16, :].astype(jnp.float32))
            return 0

        lax.fori_loop(0, X + 2, kappa, 0)

        @pl.when(c == 0)
        def _():
            for p in range(1, X + 1):
                kap[slot, p, 31:32, :] = kap[slot, p, 32:33, :]

        @pl.when(c == NC - 1)
        def _():
            for p in range(1, X + 1):
                kap[slot, p, CH + 32:CH + 33, :] = kap[slot, p, CH + 31:CH + 32, :]

        for cp in st_copies(s):
            cp.wait()

        def first(p, _):
            for r in range(8, CH + 24, 16):
                j = r + 16
                k = kap[slot, p + 1, j:j + 16, :]
                total = (6.0 * k + kap[slot, p, j:j + 16, :] + kap[slot, p + 2, j:j + 16, :]
                         + kap[slot, p + 1, j - 1:j + 15, :] + kap[slot, p + 1, j + 1:j + 17, :]
                         + jnp.where(is_first, k, rolled(k, 1)) + jnp.where(is_last, k, rolled(k, Z - 1)))
                over = 1.0 / total
                inv[slot, p, r:r + 16, :] = over
                adj[slot, p + 1, r:r + 16, :] = (2.0 * RELAX) * (
                    stw[slot, p, r:r + 16, :] - tgw[slot, p, r:r + 16, :]) * over
            return 0

        lax.fori_loop(0, X, first, 0)

        asend[s, 0] = adj[slot, 1, 16:CH + 16, :]
        asend[s, 1] = adj[slot, X, 16:CH + 16, :]
        for side in range(2):
            a_remote(s, side).start()

        @pl.when(c == 0)
        def _():
            for p in range(1, X + 1):
                adj[slot, p, 15:16, :] = jnp.zeros((1, Z), jnp.float32)

        @pl.when(c == NC - 1)
        def _():
            for p in range(1, X + 1):
                adj[slot, p, CH + 16:CH + 17, :] = jnp.zeros((1, Z), jnp.float32)

    def phase2(s):
        slot = lax.rem(s, 2)
        for side in range(2):
            a_remote(s, side).wait_recv()
        adj[slot, 0, 16:CH + 16, :] = ahalo[s, 0]
        adj[slot, X + 1, 16:CH + 16, :] = ahalo[s, 1]

        def second(p, _):
            for r in range(16, CH + 16, 16):
                j = r + 16
                k = kap[slot, p + 1, j:j + 16, :]
                a = adj[slot, p + 1, r:r + 16, :]
                ka = k * a
                am, ap = adj[slot, p, r:r + 16, :], adj[slot, p + 2, r:r + 16, :]
                bm, bp = adj[slot, p + 1, r - 1:r + 15, :], adj[slot, p + 1, r + 1:r + 17, :]
                beside = (am + ap + bm + bp
                          + jnp.where(is_first, 0.0, rolled(a, 1)) + jnp.where(is_last, 0.0, rolled(a, Z - 1)))
                beside_k = (kap[slot, p, j:j + 16, :] * am + kap[slot, p + 2, j:j + 16, :] * ap
                            + kap[slot, p + 1, j - 1:j + 15, :] * bm + kap[slot, p + 1, j + 1:j + 17, :] * bp
                            + jnp.where(is_first, 0.0, rolled(ka, 1)) + jnp.where(is_last, 0.0, rolled(ka, Z - 1)))
                t = (2.0 * RELAX) * weight * a + (RELAX * weight) * (k * beside + beside_k) * inv[slot, p, r:r + 16, :]
                term[p, r - 16:r, :] = t
            return 0

        lax.fori_loop(0, X, second, 0)
        dest = piece_of(s)

        @pl.when(dest == node)
        def _():
            row = pl.multiple_of(8 + lax.rem(s, C) * CH, 8)
            for p in range(X):
                grad[2 + p, pl.ds(row, CH), :] = term[p]

        @pl.when(dest != node)
        def _():
            for g in range(CH // 16):
                most = jnp.abs(term[0, g * 16:g * 16 + 16, :])
                for p in range(1, X):
                    most = jnp.maximum(most, jnp.abs(term[p, g * 16:g * 16 + 16, :]))
                most = jnp.maximum(jnp.max(most, axis=0, keepdims=True), 1e-20)
                sc[s, g:g + 1, :] = most * (1.0 / TOP)
                up = jnp.broadcast_to(TOP / most, (16, Z))
                for p in range(X):
                    q = jnp.round(term[p, g * 16:g * 16 + 16, :] * up)
                    qs[s, p, g * 16:g * 16 + 16, :] = q.astype(jnp.int32).astype(jnp.int16)
            for cp in q_copies(s):
                cp.start()

    def step(s, _):
        @pl.when(s < NC)
        def _():
            phase1(s)

        @pl.when(s >= 1)
        def _():
            phase2(s - 1)

        return 0

    lax.fori_loop(0, NC + 1, step, 0)

    low, high = node == 0, node == K - 1

    def g_remote(ci, side):
        row = pl.multiple_of(8 + ci * CH, 8)
        return pltpu.make_async_remote_copy(
            src_ref=grad.at[pl.ds(2 if side == 1 else X, 2), pl.ds(row, CH), :],
            dst_ref=grad.at[pl.ds(X + 2 if side == 1 else 0, 2), pl.ds(row, CH), :],
            send_sem=g_send.at[side, ci], recv_sem=g_recv.at[side, ci],
            device_id=(left if side == 1 else right, node), device_id_type=MESH)

    def row_copies(up):
        src_row, dst_row, base = (R, 0, 0) if up else (8, R + 8, 3)
        to = jnp.clip(node + (1 if up else -1), 0, K - 1)
        result = []
        for n, (src, dst, count, g) in enumerate((
                (2, 2, X, gx), (2, X + 2, 1, left), (X + 1, 1, 1, right))):
            result.append(pltpu.make_async_remote_copy(
                src_ref=grad.at[pl.ds(src, count), pl.ds(src_row, 8), :],
                dst_ref=grad.at[pl.ds(dst, count), pl.ds(dst_row, 8), :],
                send_sem=r_send.at[base + n], recv_sem=r_recv.at[base + n],
                device_id=(g, to), device_id_type=MESH))
        return result

    def gather(ci, _):
        for j in range(K - 1):
            pltpu.make_async_remote_copy(
                src_ref=qs.at[0], dst_ref=qr.at[j, ci], send_sem=q_send.at[0],
                recv_sem=q_recv.at[j, ci], device_id=(left, node), device_id_type=MESH).wait_recv()
            pltpu.make_async_remote_copy(
                src_ref=sc.at[0], dst_ref=sr.at[j, ci], send_sem=s_send.at[0],
                recv_sem=s_recv.at[j, ci], device_id=(left, node), device_id_type=MESH).wait_recv()

        def plane(p, _):
            for g in range(CH // 16):
                row = pl.multiple_of(8 + ci * CH + g * 16, 8)
                total = grad[2 + p, pl.ds(row, 16), :]
                for j in range(K - 1):
                    total += qr[j, ci, p, g * 16:g * 16 + 16, :].astype(jnp.float32) * sr[j, ci, g:g + 1, :]
                grad[2 + p, pl.ds(row, 16), :] = total
            return 0

        lax.fori_loop(0, X, plane, 0)
        for side in range(2):
            g_remote(ci, side).start()
        return 0

    lax.fori_loop(0, C, gather, 0)

    @pl.when(jnp.logical_not(high))
    def _():
        for cp in row_copies(True):
            cp.start()

    @pl.when(jnp.logical_not(low))
    def _():
        for cp in row_copies(False):
            cp.start()

    @pl.when(low)
    def _():
        grad[:, 0:8, :] = jnp.zeros((X + 4, 8, Z), jnp.float32)

    @pl.when(high)
    def _():
        grad[:, R + 8:R + 16, :] = jnp.zeros((X + 4, 8, Z), jnp.float32)

    @pl.when(jnp.logical_not(low))
    def _():
        for cp in row_copies(True):
            cp.wait_recv()

    @pl.when(jnp.logical_not(high))
    def _():
        for cp in row_copies(False):
            cp.wait_recv()

    def halo_wait(ci, _):
        for side in range(2):
            g_remote(ci, side).wait_recv()
        return 0

    lax.fori_loop(0, C, halo_wait, 0)
    scale = 1.0 / (1.0 + 6.0 * BETA)

    def smoothed(ref, p, source, r, n):
        v = ref[p, r:r + n, :]
        beside = (ref[p - 1, r:r + n, :] + ref[p + 1, r:r + n, :]
                  + ref[p, r - 1:r + n - 1, :] + ref[p, r + 1:r + n + 1, :]
                  + jnp.where(is_first[:n], 0.0, rolled(v, 1)) + jnp.where(is_last[:n], 0.0, rolled(v, Z - 1)))
        return (source + BETA * beside) * scale

    def sweep1(p, _):
        for r in range(8, R + 8, 16):
            sm1[p, r:r + 16, :] = smoothed(grad, p, grad[p, r:r + 16, :], r, 16)
        return 0

    lax.fori_loop(1, X + 3, sweep1, 0)
    keep_low = jnp.where(low, 0.0, 1.0)
    keep_high = jnp.where(high, 0.0, 1.0)

    def sweep1_rows(p, _):
        for r, keep in ((7, keep_low), (R + 8, keep_high)):
            v = grad[p, r:r + 1, :]
            wide = jnp.broadcast_to(v, (8, Z))
            beside = (grad[p - 1, r:r + 1, :] + grad[p + 1, r:r + 1, :]
                      + grad[p, r - 1:r, :] + grad[p, r + 1:r + 2, :]
                      + (jnp.where(is_first[:8], 0.0, rolled(wide, 1))
                         + jnp.where(is_last[:8], 0.0, rolled(wide, Z - 1)))[0:1])
            sm1[p, r:r + 1, :] = (v + BETA * beside) * scale * keep
        return 0

    lax.fori_loop(2, X + 2, sweep1_rows, 0)

    def sweep2(p, _):
        for r in range(8, R + 8, 16):
            out[p - 2, r - 8:r + 8, :] = smoothed(sm1, p, grad[p, r:r + 16, :], r, 16)
        return 0

    lax.fori_loop(2, X + 2, sweep2, 0)

    def drain(s, _):
        for side in range(2):
            lf_remote(s, side).wait_send()
            a_remote(s, side).wait_send()

        @pl.when(piece_of(s) != node)
        def _():
            for cp in q_copies(s):
                cp.wait_send()

        return 0

    lax.fori_loop(0, NC, drain, 0)

    def halo_drain(ci, _):
        for side in range(2):
            g_remote(ci, side).wait_send()
        return 0

    lax.fori_loop(0, C, halo_drain, 0)

    @pl.when(jnp.logical_not(high))
    def _():
        for cp in row_copies(True):
            cp.wait_send()

    @pl.when(jnp.logical_not(low))
    def _():
        for cp in row_copies(False):
            cp.wait_send()


def per_device(G, K, CH, logfield, state, target, node_index, weight_numer):
    X, Y, Z = target.shape
    R = Y // K
    CH = min(CH, R)
    C = R // CH
    NC = K * C
    f32, dma = jnp.float32, pltpu.SemaphoreType.DMA
    anywhere = pl.BlockSpec(memory_space=pl.ANY)
    scalars = pl.BlockSpec(memory_space=pltpu.SMEM)
    return pl.pallas_call(
        functools.partial(kernel, G, K, X, Y, Z, CH),
        out_shape=jax.ShapeDtypeStruct((X, R, Z), f32),
        in_specs=[anywhere, anywhere, anywhere, scalars, scalars],
        out_specs=pl.BlockSpec(memory_space=pltpu.VMEM),
        scratch_shapes=[
            pltpu.VMEM((NC, X + 2, CH + 64, Z), jnp.bfloat16),
            pltpu.VMEM((2, X, CH + 32, Z), f32),
            pltpu.VMEM((2, X, CH + 32, Z), f32),
            pltpu.VMEM((2, X + 2, CH + 64, Z), f32),
            pltpu.VMEM((2, X + 2, CH + 32, Z), f32),
            pltpu.VMEM((2, X, CH + 32, Z), f32),
            pltpu.VMEM((NC, 2, CH, Z), f32),
            pltpu.VMEM((NC, 2, CH, Z), f32),
            pltpu.VMEM((X, CH, Z), f32),
            pltpu.VMEM((NC, X, CH, Z), jnp.int16),
            pltpu.VMEM((NC, 8, Z), f32),
            pltpu.VMEM((K - 1, C, X, CH, Z), jnp.int16),
            pltpu.VMEM((K - 1, C, 8, Z), f32),
            pltpu.VMEM((X + 4, R + 16, Z), f32),
            pltpu.VMEM((X + 4, R + 16, Z), f32),
            dma((NC,)), dma((2, NC)), dma((2, NC)), dma((2,)), dma((2,)), dma((2, NC)), dma((2, NC)),
            dma((NC,)), dma((K - 1, C)), dma((NC,)), dma((K - 1, C)), dma((2, C)), dma((2, C)), dma((6,)), dma((6,)),
        ],
        compiler_params=pltpu.CompilerParams(
            collective_id=0, has_side_effects=True, vmem_limit_bytes=58 * 1024 * 1024),
    )(logfield, state, target, node_index, weight_numer)


def solution(mesh):
    in_specs = (
        P("node", "gx", None, None),
        P("node", "gx", None, None),
        P("gx", None, None),
        P("node"),
        P("node"),
    )
    return jax.shard_map(
        functools.partial(per_device, mesh.shape["gx"], mesh.shape["node"], 64), mesh=mesh,
        in_specs=in_specs, out_specs=P("gx", "node", None), check_vma=False)
```

time: 484 us -> 127 us (0.26)
  waiting for transfers between devices: 338 us -> 0 us
  Pallas kernels: 0 us -> 123 us
  other arithmetic: 95.2 us -> 0 us
  starting transfers between devices: 19.7 us -> 0 us
  between operations: 14.9 us -> 1.3 us
  local copies, waits for them, and re-layouts: 15.6 us -> 3.05 us
    psum x1 -> x0, waiting for transfers between devices: 293 us -> none  [per_device(): total = lax.psum(term, 'node')]
    pallas_call x0 -> x1, Pallas kernels: none -> 123 us  [per_device(): pl.pallas_call(functools.partial(kernel, G, K, X, Y, Z, CH), out_shape=ja...]
    mul x1 -> x0, other arithmetic: 50.8 us -> none  [per_device(): term = weight * adjoint]
    ppermute x12 -> x0, waiting for transfers between devices: 44.9 us -> none  [the longest x6 43.4 us: extended(): lax.ppermute(tail, axis, [(i, (i + 1) % count) for i in range(count)])]
    div x3 -> x0, other arithmetic: 40 us -> none  [the longest x1 33.2 us: per_device(): adjoint = relax * misfit / diagonal]
    ppermute x12 -> x0, starting transfers between devices: 19.7 us -> none  [the longest x6 16.1 us: extended(): lax.ppermute(head, axis, [((i + 1) % count, i) for i in range(count)])]
    slice x9 -> x0, local copies, waits for them, and re-layouts: 12.4 us -> none  [the longest x4 4.04 us: extended(): lax.slice_in_dim(cells, cells.shape[dim] - width, cells.shape[dim], axis=...]
  transfers between devices with their start and end apart: 13 -> 0, of which waited for: 8 -> 0; matrix products, arithmetic and copies ran while one was open for 0% -> 0% of each run, Pallas kernels for 0% -> 0%
where the time goes in v1:
time: 127 us
  Pallas kernels  123 us (97%)
  local copies, waits for them, and re-layouts  3.05 us (2%)
  between operations  1.3 us (1%)
    pallas_call x1, Pallas kernels, per_device(): pl.pallas_call(functools.partial(kernel, G, K, X, Y, Z, CH), out_shape=ja...  123 us
    unnamed x1, local copies, waits for them, and re-layouts  3.05 us

profile of v1, /device:TPU:0, one launch (start us, length us, event | category | flops | bytes accessed | tf_op | source)
XLA Modules:
  0.0 127.3 jit_solution(11450063064185495201)
XLA Ops:
  1.3 123.0 %shard_map.55 = f32[8,256,256]{2,1,0:T(8,128)} custom-call(bf16[1,8,1024,256]{3,2,1,0:T(8,128)(2,1)} %lf.1, f32[1,8,1024,256]{3,2,1,0:T(8,128)} %st.1, f32[8,1024,256]{2,1,0:T(8,128)} %tg.1, s32[1]{0:T(128)S(6)} %copy.7.ni, s32[1]{0:T(128)S(6)} %copy.8.wn), custom_call_target="tpu_custom_call" | custom-call | tf_op jit(solution)/shard_map/pallas_call | solution.py:408
  124.3 3.0 %copy.9 = f32[8,256,256]{2,1,0:T(8,128)} copy(f32[8,256,256]{2,1,0:T(8,128)} %shard_map.55) | data formatting | bytes 4194304

commit v2 on v1

--- a/solution.py
+++ b/solution.py
@@ -11,6 +11,7 @@
 RELAX = 2.0 / 3.0
 BETA = 1.0
 TOP = 32767.0
+LAG = 2
 MESH = pl.DeviceIdType.MESH
 
 
@@ -37,8 +38,22 @@
     for k in range(1, K):
         pl.semaphore_signal(barrier, inc=1, device_id=(gx, lax.rem(node + k, K)), device_id_type=MESH)
 
+    inner = (node > 0) & (node < K - 1)
+    lag = jnp.where(inner, LAG, 0)
+    orders = [sorted(range(K), key=lambda d: (-abs(d - p) if d != p else 1, -d)) for p in range(K)]
+    turns = []
+    for i in range(K):
+        turn = jnp.int32(orders[0][i])
+        for p in range(1, K):
+            turn = jnp.where(node == p, orders[p][i], turn)
+        turns.append(turn)
+
     def piece_of(s):
-        return lax.rem(node + K - 1 - s // C + K, K)
+        i = s // C
+        piece = turns[0]
+        for n in range(1, K):
+            piece = jnp.where(i == n, turns[n], piece)
+        return piece
 
     def chunk_of(s):
         return piece_of(s) * C + lax.rem(s, C)
@@ -86,15 +101,16 @@
     def q_copies(s):
         dest = piece_of(s)
         ci = lax.rem(s, C)
-        slot = jnp.where(node < dest, node, node - 1)
-        slot = jnp.clip(slot, 0, K - 2)
+        upward = dest > node
+        slot = jnp.where(dest == node - 1, K, dest)
+        to = jnp.clip(jnp.where(upward, node + 1, node - 1), 0, K - 1)
         return (
             pltpu.make_async_remote_copy(
                 src_ref=qs.at[s], dst_ref=qr.at[slot, ci], send_sem=q_send.at[s],
-                recv_sem=q_recv.at[slot, ci], device_id=(gx, dest), device_id_type=MESH),
+                recv_sem=q_recv.at[slot, ci], device_id=(gx, to), device_id_type=MESH),
             pltpu.make_async_remote_copy(
                 src_ref=sc.at[s], dst_ref=sr.at[slot, ci], send_sem=s_send.at[s],
-                recv_sem=s_recv.at[slot, ci], device_id=(gx, dest), device_id_type=MESH))
+                recv_sem=s_recv.at[slot, ci], device_id=(gx, to), device_id_type=MESH))
 
     index = ni[0]
     half = jnp.float32(0.5 * math.cos(0.0))
@@ -113,6 +129,14 @@
     for s in range(2):
         for side in range(2):
             lf_remote(s, side).start()
+
+    def arrived(slot, ci):
+        pltpu.make_async_remote_copy(
+            src_ref=qs.at[0], dst_ref=qr.at[slot, ci], send_sem=q_send.at[0],
+            recv_sem=q_recv.at[slot, ci], device_id=(left, node), device_id_type=MESH).wait_recv()
+        pltpu.make_async_remote_copy(
+            src_ref=sc.at[0], dst_ref=sr.at[slot, ci], send_sem=s_send.at[0],
+            recv_sem=s_recv.at[slot, ci], device_id=(left, node), device_id_type=MESH).wait_recv()
 
     def phase1(s):
         slot = lax.rem(s, 2)
@@ -185,6 +209,7 @@
 
     def phase2(s):
         slot = lax.rem(s, 2)
+        place = lax.rem(s, LAG + 1)
         for side in range(2):
             a_remote(s, side).wait_recv()
         adj[slot, 0, 16:CH + 16, :] = ahalo[s, 0]
@@ -204,29 +229,45 @@
                             + kap[slot, p + 1, j - 1:j + 15, :] * bm + kap[slot, p + 1, j + 1:j + 17, :] * bp
                             + jnp.where(is_first, 0.0, rolled(ka, 1)) + jnp.where(is_last, 0.0, rolled(ka, Z - 1)))
                 t = (2.0 * RELAX) * weight * a + (RELAX * weight) * (k * beside + beside_k) * inv[slot, p, r:r + 16, :]
-                term[p, r - 16:r, :] = t
+                term[place, p, r - 16:r, :] = t
             return 0
 
         lax.fori_loop(0, X, second, 0)
+
+    def phase3(s):
+        place = lax.rem(s, LAG + 1)
         dest = piece_of(s)
+        ci = lax.rem(s, C)
+
+        @pl.when((dest != node) & inner)
+        def _():
+            arrived(dest, ci)
+
+            def add(p, _):
+                for g in range(CH // 16):
+                    rows = slice(g * 16, g * 16 + 16)
+                    term[place, p, rows, :] += qr[dest, ci, p, rows, :].astype(jnp.float32) * sr[dest, ci, g:g + 1, :]
+                return 0
+
+            lax.fori_loop(0, X, add, 0)
 
         @pl.when(dest == node)
         def _():
             row = pl.multiple_of(8 + lax.rem(s, C) * CH, 8)
             for p in range(X):
-                grad[2 + p, pl.ds(row, CH), :] = term[p]
+                grad[2 + p, pl.ds(row, CH), :] = term[place, p]
 
         @pl.when(dest != node)
         def _():
             for g in range(CH // 16):
-                most = jnp.abs(term[0, g * 16:g * 16 + 16, :])
+                most = jnp.abs(term[place, 0, g * 16:g * 16 + 16, :])
                 for p in range(1, X):
-                    most = jnp.maximum(most, jnp.abs(term[p, g * 16:g * 16 + 16, :]))
+                    most = jnp.maximum(most, jnp.abs(term[place, p, g * 16:g * 16 + 16, :]))
                 most = jnp.maximum(jnp.max(most, axis=0, keepdims=True), 1e-20)
                 sc[s, g:g + 1, :] = most * (1.0 / TOP)
                 up = jnp.broadcast_to(TOP / most, (16, Z))
                 for p in range(X):
-                    q = jnp.round(term[p, g * 16:g * 16 + 16, :] * up)
+                    q = jnp.round(term[place, p, g * 16:g * 16 + 16, :] * up)
                     qs[s, p, g * 16:g * 16 + 16, :] = q.astype(jnp.int32).astype(jnp.int16)
             for cp in q_copies(s):
                 cp.start()
@@ -236,13 +277,17 @@
         def _():
             phase1(s)
 
-        @pl.when(s >= 1)
+        @pl.when((s >= 1) & (s < NC + 1))
         def _():
             phase2(s - 1)
 
-        return 0
-
-    lax.fori_loop(0, NC + 1, step, 0)
+        @pl.when((s >= 1 + lag) & (s < NC + 1 + lag))
+        def _():
+            phase3(s - 1 - lag)
+
+        return 0
+
+    lax.fori_loop(0, NC + 1 + LAG, step, 0)
 
     low, high = node == 0, node == K - 1
 
@@ -268,24 +313,26 @@
         return result
 
     def gather(ci, _):
-        for j in range(K - 1):
-            pltpu.make_async_remote_copy(
-                src_ref=qs.at[0], dst_ref=qr.at[j, ci], send_sem=q_send.at[0],
-                recv_sem=q_recv.at[j, ci], device_id=(left, node), device_id_type=MESH).wait_recv()
-            pltpu.make_async_remote_copy(
-                src_ref=sc.at[0], dst_ref=sr.at[j, ci], send_sem=s_send.at[0],
-                recv_sem=s_recv.at[j, ci], device_id=(left, node), device_id_type=MESH).wait_recv()
-
-        def plane(p, _):
-            for g in range(CH // 16):
-                row = pl.multiple_of(8 + ci * CH + g * 16, 8)
-                total = grad[2 + p, pl.ds(row, 16), :]
-                for j in range(K - 1):
-                    total += qr[j, ci, p, g * 16:g * 16 + 16, :].astype(jnp.float32) * sr[j, ci, g:g + 1, :]
-                grad[2 + p, pl.ds(row, 16), :] = total
-            return 0
-
-        lax.fori_loop(0, X, plane, 0)
+        def add(slot):
+            arrived(slot, ci)
+
+            def plane(p, _):
+                for g in range(CH // 16):
+                    row = pl.multiple_of(8 + ci * CH + g * 16, 8)
+                    grad[2 + p, pl.ds(row, 16), :] += (
+                        qr[slot, ci, p, g * 16:g * 16 + 16, :].astype(jnp.float32) * sr[slot, ci, g:g + 1, :])
+                return 0
+
+            lax.fori_loop(0, X, plane, 0)
+
+        @pl.when(node > 0)
+        def _():
+            add(node)
+
+        @pl.when(node < K - 1)
+        def _():
+            add(jnp.int32(K))
+
         for side in range(2):
             g_remote(ci, side).start()
         return 0
@@ -419,15 +466,15 @@
             pltpu.VMEM((2, X, CH + 32, Z), f32),
             pltpu.VMEM((NC, 2, CH, Z), f32),
             pltpu.VMEM((NC, 2, CH, Z), f32),
-            pltpu.VMEM((X, CH, Z), f32),
+            pltpu.VMEM((LAG + 1, X, CH, Z), f32),
             pltpu.VMEM((NC, X, CH, Z), jnp.int16),
             pltpu.VMEM((NC, 8, Z), f32),
-            pltpu.VMEM((K - 1, C, X, CH, Z), jnp.int16),
-            pltpu.VMEM((K - 1, C, 8, Z), f32),
+            pltpu.VMEM((K + 1, C, X, CH, Z), jnp.int16),
+            pltpu.VMEM((K + 1, C, 8, Z), f32),
             pltpu.VMEM((X + 4, R + 16, Z), f32),
             pltpu.VMEM((X + 4, R + 16, Z), f32),
             dma((NC,)), dma((2, NC)), dma((2, NC)), dma((2,)), dma((2,)), dma((2, NC)), dma((2, NC)),
-            dma((NC,)), dma((K - 1, C)), dma((NC,)), dma((K - 1, C)), dma((2, C)), dma((2, C)), dma((6,)), dma((6,)),
+            dma((NC,)), dma((K + 1, C)), dma((NC,)), dma((K + 1, C)), dma((2, C)), dma((2, C)), dma((6,)), dma((6,)),
         ],
         compiler_params=pltpu.CompilerParams(
             collective_id=0, has_side_effects=True, vmem_limit_bytes=58 * 1024 * 1024),

time: 127 us -> 109 us (0.86)
  Pallas kernels: 123 us -> 105 us
    pallas_call x1, Pallas kernels: 123 us -> 105 us  [per_device(): pl.pallas_call(functools.partial(kernel, G, K, X, Y, Z, CH), out_shape=ja...]
where the time goes in v2:
time: 109 us
  Pallas kernels  105 us (96%)
  local copies, waits for them, and re-layouts  3.05 us (3%)
  between operations  1.3 us (1%)
    pallas_call x1, Pallas kernels, per_device(): pl.pallas_call(functools.partial(kernel, G, K, X, Y, Z, CH), out_shape=ja...  105 us
    unnamed x1, local copies, waits for them, and re-layouts  3.05 us

profile of v2, /device:TPU:0, one launch (start us, length us, event | category | flops | bytes accessed | tf_op | source)
XLA Modules:
  0.0 109.3 jit_solution(6098292668713046108)
XLA Ops:
  1.3 105.0 %shard_map.55 = f32[8,256,256]{2,1,0:T(8,128)} custom-call(bf16[1,8,1024,256]{3,2,1,0:T(8,128)(2,1)} %lf.1, f32[1,8,1024,256]{3,2,1,0:T(8,128)} %st.1, f32[8,1024,256]{2,1,0:T(8,128)} %tg.1, s32[1]{0:T(128)S(6)} %copy.7.ni, s32[1]{0:T(128)S(6)} %copy.8.wn), custom_call_target="tpu_custom_call" | custom-call | tf_op jit(solution)/shard_map/pallas_call | solution.py:455
  106.3 3.0 %copy.9 = f32[8,256,256]{2,1,0:T(8,128)} copy(f32[8,256,256]{2,1,0:T(8,128)} %shard_map.55) | data formatting | bytes 4194304

commit v3 on v2

--- a/solution.py
+++ b/solution.py
@@ -312,7 +312,7 @@
                 device_id=(g, to), device_id_type=MESH))
         return result
 
-    def gather(ci, _):
+    def gather(ci):
         def add(slot):
             arrived(slot, ci)
 
@@ -335,44 +335,7 @@
 
         for side in range(2):
             g_remote(ci, side).start()
-        return 0
-
-    lax.fori_loop(0, C, gather, 0)
-
-    @pl.when(jnp.logical_not(high))
-    def _():
-        for cp in row_copies(True):
-            cp.start()
-
-    @pl.when(jnp.logical_not(low))
-    def _():
-        for cp in row_copies(False):
-            cp.start()
-
-    @pl.when(low)
-    def _():
-        grad[:, 0:8, :] = jnp.zeros((X + 4, 8, Z), jnp.float32)
-
-    @pl.when(high)
-    def _():
-        grad[:, R + 8:R + 16, :] = jnp.zeros((X + 4, 8, Z), jnp.float32)
-
-    @pl.when(jnp.logical_not(low))
-    def _():
-        for cp in row_copies(True):
-            cp.wait_recv()
-
-    @pl.when(jnp.logical_not(high))
-    def _():
-        for cp in row_copies(False):
-            cp.wait_recv()
-
-    def halo_wait(ci, _):
-        for side in range(2):
-            g_remote(ci, side).wait_recv()
-        return 0
-
-    lax.fori_loop(0, C, halo_wait, 0)
+
     scale = 1.0 / (1.0 + 6.0 * BETA)
 
     def smoothed(ref, p, source, r, n):
@@ -382,12 +345,24 @@
                   + jnp.where(is_first[:n], 0.0, rolled(v, 1)) + jnp.where(is_last[:n], 0.0, rolled(v, Z - 1)))
         return (source + BETA * beside) * scale
 
-    def sweep1(p, _):
-        for r in range(8, R + 8, 16):
-            sm1[p, r:r + 16, :] = smoothed(grad, p, grad[p, r:r + 16, :], r, 16)
-        return 0
-
-    lax.fori_loop(1, X + 3, sweep1, 0)
+    def sweep1(first, last):
+        def plane(p, _):
+            for r in range(first + 8, last + 8, 16):
+                sm1[p, r:r + 16, :] = smoothed(grad, p, grad[p, r:r + 16, :], r, 16)
+            return 0
+
+        if first < last:
+            lax.fori_loop(1, X + 3, plane, 0)
+
+    def sweep2(first, last):
+        def plane(p, _):
+            for r in range(first + 8, last + 8, 16):
+                out[p - 2, r - 8:r + 8, :] = smoothed(sm1, p, grad[p, r:r + 16, :], r, 16)
+            return 0
+
+        if first < last:
+            lax.fori_loop(2, X + 2, plane, 0)
+
     keep_low = jnp.where(low, 0.0, 1.0)
     keep_high = jnp.where(high, 0.0, 1.0)
 
@@ -402,14 +377,57 @@
             sm1[p, r:r + 1, :] = (v + BETA * beside) * scale * keep
         return 0
 
+    @pl.when(low)
+    def _():
+        grad[:, 0:8, :] = jnp.zeros((X + 4, 8, Z), jnp.float32)
+
+    @pl.when(high)
+    def _():
+        grad[:, R + 8:R + 16, :] = jnp.zeros((X + 4, 8, Z), jnp.float32)
+
+    done1, done2 = 16, 32
+    for ci in range(C):
+        gather(jnp.int32(ci))
+        if ci == 0:
+            @pl.when(jnp.logical_not(low))
+            def _():
+                for cp in row_copies(False):
+                    cp.start()
+
+        if ci == C - 1:
+            @pl.when(jnp.logical_not(high))
+            def _():
+                for cp in row_copies(True):
+                    cp.start()
+
+        if ci >= 1:
+            for side in range(2):
+                g_remote(jnp.int32(ci - 1), side).wait_recv()
+            upto = max(done1, ci * CH - 16)
+            sweep1(done1, upto)
+            done1 = upto
+            upto = max(done2, ci * CH - 32)
+            sweep2(done2, upto)
+            done2 = upto
+
+    for side in range(2):
+        g_remote(jnp.int32(C - 1), side).wait_recv()
+
+    @pl.when(jnp.logical_not(low))
+    def _():
+        for cp in row_copies(True):
+            cp.wait_recv()
+
+    @pl.when(jnp.logical_not(high))
+    def _():
+        for cp in row_copies(False):
+            cp.wait_recv()
+
+    sweep1(0, 16)
+    sweep1(done1, R)
     lax.fori_loop(2, X + 2, sweep1_rows, 0)
-
-    def sweep2(p, _):
-        for r in range(8, R + 8, 16):
-            out[p - 2, r - 8:r + 8, :] = smoothed(sm1, p, grad[p, r:r + 16, :], r, 16)
-        return 0
-
-    lax.fori_loop(2, X + 2, sweep2, 0)
+    sweep2(0, 32)
+    sweep2(done2, R)
 
     def drain(s, _):
         for side in range(2):

time: 109 us -> 109 us (level)
  no operation moved by 1% of the time
where the time goes in v3:
time: 109 us
  Pallas kernels  105 us (96%)
  local copies, waits for them, and re-layouts  3.05 us (3%)
  between operations  1.3 us (1%)
    pallas_call x1, Pallas kernels, per_device(): pl.pallas_call(functools.partial(kernel, G, K, X, Y, Z, CH), out_shape=ja...  105 us
    unnamed x1, local copies, waits for them, and re-layouts  3.05 us

profile of v3, /device:TPU:0, one launch (start us, length us, event | category | flops | bytes accessed | tf_op | source)
XLA Modules:
  0.0 109.2 jit_solution(11980621327336142827)
XLA Ops:
  1.3 104.8 %shard_map.55 = f32[8,256,256]{2,1,0:T(8,128)} custom-call(bf16[1,8,1024,256]{3,2,1,0:T(8,128)(2,1)} %lf.1, f32[1,8,1024,256]{3,2,1,0:T(8,128)} %st.1, f32[8,1024,256]{2,1,0:T(8,128)} %tg.1, s32[1]{0:T(128)S(6)} %copy.7.ni, s32[1]{0:T(128)S(6)} %copy.8.wn), custom_call_target="tpu_custom_call" | custom-call | tf_op jit(solution)/shard_map/pallas_call | solution.py:473
  106.2 3.0 %copy.9 = f32[8,256,256]{2,1,0:T(8,128)} copy(f32[8,256,256]{2,1,0:T(8,128)} %shard_map.55) | data formatting | bytes 4194304

commit v4 on v3

--- a/solution.py
+++ b/solution.py
@@ -142,12 +142,6 @@
         slot = lax.rem(s, 2)
         c = chunk_of(s)
 
-        @pl.when(s + 2 < NC)
-        def _():
-            lf_local(s + 2).start()
-            for side in range(2):
-                lf_remote(s + 2, side).start()
-
         @pl.when(s + 1 < NC)
         def _():
             for cp in st_copies(s + 1):
@@ -196,6 +190,12 @@
         asend[s, 1] = adj[slot, X, 16:CH + 16, :]
         for side in range(2):
             a_remote(s, side).start()
+
+        @pl.when(s + 2 < NC)
+        def _():
+            lf_local(s + 2).start()
+            for side in range(2):
+                lf_remote(s + 2, side).start()
 
         @pl.when(c == 0)
         def _():

time: 109 us -> 110 us (level)
  no operation moved by 1% of the time
where the time goes in v4:
time: 110 us; the launch traced here: 109 us
  Pallas kernels  105 us (95%)
  local copies, waits for them, and re-layouts  3.05 us (3%)
  between operations  1.3 us (1%)
    pallas_call x1, Pallas kernels, per_device(): pl.pallas_call(functools.partial(kernel, G, K, X, Y, Z, CH), out_shape=ja...  105 us
    unnamed x1, local copies, waits for them, and re-layouts  3.05 us

profile of v4, /device:TPU:0, one launch (start us, length us, event | category | flops | bytes accessed | tf_op | source)
XLA Modules:
  0.0 109.4 jit_solution(15461752454299919522)
XLA Ops:
  1.3 105.1 %shard_map.55 = f32[8,256,256]{2,1,0:T(8,128)} custom-call(bf16[1,8,1024,256]{3,2,1,0:T(8,128)(2,1)} %lf.1, f32[1,8,1024,256]{3,2,1,0:T(8,128)} %st.1, f32[8,1024,256]{2,1,0:T(8,128)} %tg.1, s32[1]{0:T(128)S(6)} %copy.7.ni, s32[1]{0:T(128)S(6)} %copy.8.wn), custom_call_target="tpu_custom_call" | custom-call | tf_op jit(solution)/shard_map/pallas_call | solution.py:473
  106.4 3.0 %copy.9 = f32[8,256,256]{2,1,0:T(8,128)} copy(f32[8,256,256]{2,1,0:T(8,128)} %shard_map.55) | data formatting | bytes 4194304

commit v5 on v4

--- a/solution.py
+++ b/solution.py
@@ -40,7 +40,7 @@
 
     inner = (node > 0) & (node < K - 1)
     lag = jnp.where(inner, LAG, 0)
-    orders = [sorted(range(K), key=lambda d: (-abs(d - p) if d != p else 1, -d)) for p in range(K)]
+    orders = [sorted(range(K), key=lambda d: (-abs(d - p) if d != p else 1, -abs(2 * d - K + 1))) for p in range(K)]
     turns = []
     for i in range(K):
         turn = jnp.int32(orders[0][i])

time: 110 us -> 103 us (0.936)
  the two profiles are of different devices: /device:TPU:0 before, /device:TPU:8 now
where the time goes in v5:
time: 103 us
  Pallas kernels  98.9 us (96%)
  local copies, waits for them, and re-layouts  3.05 us (3%)
  between operations  1.3 us (1%)
    pallas_call x1, Pallas kernels, per_device(): pl.pallas_call(functools.partial(kernel, G, K, X, Y, Z, CH), out_shape=ja...  98.9 us
    unnamed x1, local copies, waits for them, and re-layouts  3.05 us

profile of v5, /device:TPU:8, one launch (start us, length us, event | category | flops | bytes accessed | tf_op | source)
XLA Modules:
  0.0 103.2 jit_solution(11445115780264722682)
XLA Ops:
  1.3 98.9 %shard_map.55 = f32[8,256,256]{2,1,0:T(8,128)} custom-call(bf16[1,8,1024,256]{3,2,1,0:T(8,128)(2,1)} %lf.1, f32[1,8,1024,256]{3,2,1,0:T(8,128)} %st.1, f32[8,1024,256]{2,1,0:T(8,128)} %tg.1, s32[1]{0:T(128)S(6)} %copy.7.ni, s32[1]{0:T(128)S(6)} %copy.8.wn), custom_call_target="tpu_custom_call" | custom-call | tf_op jit(solution)/shard_map/pallas_call | solution.py:473
  100.2 3.0 %copy.9 = f32[8,256,256]{2,1,0:T(8,128)} copy(f32[8,256,256]{2,1,0:T(8,128)} %shard_map.55) | data formatting | bytes 4194304
